TPU v7x, 256 devices: a whole 4x4x8 slice. The times are simulated.
256 devices in a mesh: dom: 64 (over z, x, core), rep: 4 (over y).
Axes of the slice: x: 4, y: 4, z: 8, core: 2. Of those that a mesh axis runs over, the one named last changes fastest.
Arguments:
- history: bfloat16 [131072, 256], P('dom'), may hold values from -6 to 6
- batch_ids: int32 [262144], P(('dom', 'rep')), may hold values from 0 to 2047
- halo_ids: int32 [256, 64, 32], P(('dom', 'rep')), may hold values from 0 to 2047
- halo_counts: int32 [256, 64], P(('dom', 'rep')), may hold values from 1 to 32, as said below
- adj_local: bfloat16 [262144, 1024], P(('dom', 'rep')), may hold values from -0.109375 to 0.109375
- adj_halo: bfloat16 [262144, 2048], P(('dom', 'rep')), may hold values from -0.109375 to 0.109375
- weight: bfloat16 [256, 256], replicated, may hold values from -0.375 to 0.375
- cotangent: bfloat16 [262144, 256], P(('dom', 'rep')), may hold values from -6 to 6
Outputs:
- layer_out: bfloat16 [262144, 256], P(('dom', 'rep'))
- grad_weight: float32 [256, 256], replicated
- history_grad: float32 [131072, 256], P('dom')
Inputs may be any that keep to these rules, and one draw needn't show every extreme that they name: `halo_counts`: every device takes from every owner between 1 and 32 rows; for some owners every device takes exactly 32. `halo_ids`: rows of the owner's history; slots at or past the used count are unused. `batch_ids`: rows of the device's own partition's history; may repeat.
All inputs are finite; a program needn't handle non-finite values.
Results may differ from a plain program's by a relative error of at most 0.0065.
Values may be sent and summed in bfloat16 or wider, within the bound.
No kernel may reach another device: no remote copies, remote signals or barrier semaphores. Data moves between devices by JAX's collectives and lax.ppermute only.
A program may use at most 64 MiB of HBM per device.

v0:
```python
import jax
import jax.numpy as jnp
from jax import lax
from jax.sharding import PartitionSpec as P


def body(history, batch_ids, halo_ids, halo_counts, adj_local, adj_halo, weight, cotangent):
    owners = lax.axis_size("dom")
    replicas = lax.axis_size("rep")
    batch_rows = batch_ids.shape[0]
    slots_per = halo_ids.shape[2]
    feature_width = history.shape[1]
    inputs = history[batch_ids]
    requests = halo_ids.reshape(owners, 1, slots_per)
    asked_ids = lax.all_to_all(requests, "dom", split_axis=0, concat_axis=0, tiled=True)
    fetched = history[asked_ids]
    returned = lax.all_to_all(fetched, "dom", split_axis=0, concat_axis=0, tiled=True)
    asked_ids, fetched_rows = (asked_ids, returned)
    halo_rows = fetched_rows.reshape(owners * slots_per, feature_width)
    live_slots = (
        jnp.arange(slots_per, dtype=jnp.int32)[None, :] < halo_counts.reshape(owners, 1)
    ).reshape(-1)
    masked = adj_halo * live_slots.astype(jnp.bfloat16)[None, :]
    summed = jnp.dot(adj_local, inputs, preferred_element_type=jnp.float32) + jnp.dot(
        masked, halo_rows, preferred_element_type=jnp.float32
    )
    agg = summed.astype(jnp.bfloat16)
    pre_act = jnp.dot(agg, weight, preferred_element_type=jnp.float32)
    gate_sig = jax.nn.sigmoid(pre_act)
    layer_out = (pre_act * gate_sig).astype(jnp.bfloat16)
    grad_pre = (
        cotangent.astype(jnp.float32) * gate_sig * (1.0 + pre_act * (1.0 - gate_sig))
    ).astype(jnp.bfloat16)
    weight_part = lax.dot_general(
        agg, grad_pre, (((0,), (0,)), ((), ())), preferred_element_type=jnp.float32
    )
    total_rows = batch_rows * owners * replicas
    grad_weight = lax.psum(weight_part, ("dom", "rep")) / jnp.sqrt(jnp.float32(total_rows))
    grad_agg = lax.dot_general(
        grad_pre, weight, (((1,), (1,)), ((), ())), preferred_element_type=jnp.float32
    ).astype(jnp.bfloat16)
    grad_inputs = lax.dot_general(
        adj_local, grad_agg, (((0,), (0,)), ((), ())), preferred_element_type=jnp.float32
    ).astype(jnp.bfloat16)
    grad_halo = lax.dot_general(
        masked, grad_agg, (((0,), (0,)), ((), ())), preferred_element_type=jnp.float32
    ).astype(jnp.bfloat16)
    arrived = lax.all_to_all(
        grad_halo.reshape(owners, slots_per, feature_width),
        "dom",
        split_axis=0,
        concat_axis=0,
        tiled=True,
    )
    arrived_rows = arrived.reshape(owners * slots_per, feature_width)
    asked_flat = asked_ids.reshape(-1)
    empty_table = jnp.zeros((history.shape[0], feature_width), jnp.float32)
    grad_table = empty_table.at[batch_ids].add(grad_inputs.astype(jnp.float32))
    grad_table = grad_table.at[asked_flat].add(arrived_rows.astype(jnp.float32))
    history_grad = lax.psum(grad_table, "rep")
    return (layer_out, grad_weight, history_grad)


def solution(mesh):
    return jax.shard_map(
        body,
        mesh=mesh,
        in_specs=(
            P("dom", None),
            P(("dom", "rep")),
            P(("dom", "rep"), None, None),
            P(("dom", "rep"), None),
            P(("dom", "rep"), None),
            P(("dom", "rep"), None),
            P(),
            P(("dom", "rep"), None),
        ),
        out_specs=(P(("dom", "rep"), None), P(), P("dom", None)),
        check_vma=False,
    )
```

profile of v0, /device:TPU:1, one launch (start us, length us, event | category | flops | bytes accessed | tf_op | source)
XLA Modules:
  0.0 426.3 jit_solution(2159902217912049658)
XLA Ops:
  7.2 0.0 copy-start
  7.2 0.9 copy.17
  8.1 22.2 %all_to_all.15 = s32[64,1,32]{2,1,0:T(1,128)S(1)} all-to-all(s32[64,1,32]{2,1,0:T(1,128)S(1)} %bitcast.33), channel_id=1, replica_groups=mesh['dom'=64,'rep'=4] {'dom'}, dimensions={0} | all-to-all | bytes 16384 | tf_op jit(solution)/shard_map/all_to_all | solution.py:15
  30.3 0.5 broadcast.51
  30.8 0.8 fusion.19
  31.6 0.1 reshape.83
  31.7 9.9 %gather_fusion.1 = bf16[2048,256]{1,0:T(8,128)(2,1)} fusion(bf16[2048,256]{1,0:T(8,128)(2,1)} %param.8, s32[2048]{0:T(1024)S(1)} %broadcast_clamp_fusion), kind=kCustom, calls=%fused_computation.1 | custom fusion | bytes 2105344 | tf_op jit(solution)/shard_map/gather | solution.py:16
  41.6 0.0 copy-start.8
  41.6 0.0 copy-start.7
  41.6 0.0 copy-start.1
  41.6 5.7 %all-to-all-start.1 = ((bf16[64,1,32,256]{3,2,1,0:T(8,128)(2,1)}), bf16[64,1,32,256]{3,2,1,0:T(8,128)(2,1)}, u32[]{:S(2)}, u32[]{:S(2)}) async-start(bf16[64,1,32,256]{3,2,1,0:T(8,128)(2,1)} %bitcast.31), calls=%async_computation.1 | async-start | bytes 2097152 | tf_op jit(solution)/shard_map/all_to_all | solution.py:17
  47.3 0.0 copy-done.8
  47.3 0.1 fusion.18
  47.4 0.1 reshape.71
  47.5 0.0 copy-done.7
  47.5 0.0 copy-done.1
  47.5 5.0 %gather_fusion = bf16[1024,256]{1,0:T(8,128)(2,1)} fusion(bf16[2048,256]{1,0:T(8,128)(2,1)S(1)} %copy-done.1, s32[1024]{0:T(1024)S(1)} %get-tuple-element.8), kind=kCustom, calls=%fused_computation | custom fusion | bytes 1052672 | tf_op jit(solution)/shard_map/gather | solution.py:13
  52.5 22.9 %all-to-all-done.1 = bf16[64,1,32,256]{3,2,1,0:T(8,128)(2,1)} async-done(((bf16[64,1,32,256]{3,2,1,0:T(8,128)(2,1)}), bf16[64,1,32,256]{3,2,1,0:T(8,128)(2,1)}, u32[]{:S(2)}, u32[]{:S(2)}) %all-to-all-start.1) | async-done | bytes 1048608 | tf_op jit(solution)/shard_map/all_to_all | solution.py:17
  75.4 0.0 copy-start.5
  75.4 3.8 fusion.2
  79.2 0.0 copy-done
  79.2 0.0 copy-done.5
  79.2 0.0 copy-start.6
  79.2 0.0 copy-start.10
  79.2 0.8 fusion.14
  80.0 0.1 copy-done.6
  80.1 0.2 copy-done.10
  80.3 0.0 copy-start.4
  80.3 0.0 copy-start.9
  80.4 1.5 multiply_convert_fusion
  81.9 0.0 copy-done.4
  81.9 0.0 copy-start.3
  81.9 0.8 copy-done.3
  82.7 0.3 convolution_convert_fusion
  83.0 0.1 copy-done.9
  83.1 0.0 copy-start.2
  83.1 2.4 fusion.4
  85.5 0.0 copy-done.2
  85.5 6.4 %all-to-all-start.2 = ((bf16[64,32,256]{2,1,0:T(8,128)(2,1)}), bf16[64,32,256]{2,1,0:T(8,128)(2,1)S(1)}, u32[]{:S(2)}, u32[]{:S(2)}) async-start(bf16[64,32,256]{2,1,0:T(8,128)(2,1)} %bitcast.32), calls=%async_computation.2 | async-start | bytes 2097152 | tf_op jit(solution)/shard_map/all_to_all | solution.py:48
  92.0 0.0 all-reduce.3.cloned.1.call-start
  92.0 0.1 reshape.69
  92.1 2.2 fusion.20
  94.3 0.0 all-reduce.3.cloned.1.call-update
  94.3 0.2 all-reduce.5.cloned.1.call-start
  94.6 2.7 fusion.13
  97.3 2.6 copy.20
  99.9 7.9 %scatter_custom_fusion = f32[2048,256]{1,0:T(8,128)} fusion(s32[1024]{0:T(1024)S(1)} %get-tuple-element.7, f32[1024,256]{1,0:T(8,128)} %copy.20, f32[]{:T(128)} %constant.1.clone.1), kind=kCustom, calls=%fused_computation.20 | custom fusion | flops 262144 | bytes 2097664 | tf_op jit(solution)/shard_map/scatter-add | solution.py:58
  107.8 12.1 %all-to-all-done.2 = bf16[64,32,256]{2,1,0:T(8,128)(2,1)S(1)} async-done(((bf16[64,32,256]{2,1,0:T(8,128)(2,1)}), bf16[64,32,256]{2,1,0:T(8,128)(2,1)S(1)}, u32[]{:S(2)}, u32[]{:S(2)}) %all-to-all-start.2) | async-done | bytes 1048608 | tf_op jit(solution)/shard_map/all_to_all | solution.py:48
  120.0 14.5 %scatter_custom_fusion.1 = f32[2048,256]{1,0:T(8,128)} fusion(f32[2048,256]{1,0:T(8,128)} %scatter_custom_fusion, s32[2048]{0:T(1024)S(1)} %bitcast.34, bf16[2048,256]{1,0:T(8,128)(2,1)S(1)} %bitcast.30), kind=kCustom, calls=%fused_computation.9 | custom fusion | flops 1048576 | bytes 3145728 | tf_op jit(solution)/shard_map/scatter-add | solution.py:59
  134.5 0.0 all-reduce.5.cloned.1.call-update
  134.5 215.0 %all-reduce.3.cloned.1.call-done = f32[256,256]{1,0:T(8,128)} async-done(((f32[256,256]{1,0:T(8,128)}), f32[256,256]{1,0:T(8,128)}) %all-reduce.3.cloned.1.call-update) | async-done | bytes 262160 | tf_op jit(solution)/shard_map/psum | solution.py:38
  349.5 1.7 broadcast_multiply_fusion
  351.2 65.2 %all-reduce.5.cloned.1.call-done = f32[2048,256]{1,0:T(8,128)} async-done(((f32[2048,256]{1,0:T(8,128)}), f32[2048,256]{1,0:T(8,128)}) %all-reduce.5.cloned.1.call-update) | async-done | bytes 2097168 | tf_op jit(solution)/shard_map/psum | solution.py:60
  416.4 3.0 copy.25
  (3 shorter events, 0.0 us)
Async XLA Ops:
  7.2 72.0 %copy-start = (bf16[1024,1024]{1,0:T(8,128)(2,1)S(1)}, bf16[1024,1024]{1,0:T(8,128)(2,1)}, u32[]{:S(2)}) copy-start(bf16[1024,1024]{1,0:T(8,128)(2,1)} %param.12) | copy-start | bytes 6291460
  41.6 5.7 %copy-start.8 = (s32[1,64]{1,0:T(1,128)S(1)}, s32[1,64]{1,0:T(1,128)}, u32[]{:S(2)}) copy-start(s32[1,64]{1,0:T(1,128)} %param.11) | copy-start | bytes 772
  41.6 5.9 %copy-start.7 = (s32[1024]{0:T(1024)S(1)}, s32[1024]{0:T(1024)}, u32[]{:S(2)}) copy-start(s32[1024]{0:T(1024)} %param.9) | copy-start | bytes 12292
  41.6 5.9 %copy-start.1 = (bf16[2048,256]{1,0:T(8,128)(2,1)S(1)}, bf16[2048,256]{1,0:T(8,128)(2,1)}, u32[]{:S(2)}) copy-start(bf16[2048,256]{1,0:T(8,128)(2,1)} %param.8) | copy-start | bytes 3145732
  41.6 33.8 %all-to-all-start.1 = ((bf16[64,1,32,256]{3,2,1,0:T(8,128)(2,1)}), bf16[64,1,32,256]{3,2,1,0:T(8,128)(2,1)}, u32[]{:S(2)}, u32[]{:S(2)}) async-start(bf16[64,1,32,256]{3,2,1,0:T(8,128)(2,1)} %bitcast.31), calls=%async_computation.1 | async-start | bytes 2097152 | tf_op jit(solution)/shard_map/all_to_all | solution.py:17
  75.4 3.9 copy-start.5
  79.2 0.9 copy-start.6
  79.2 1.1 copy-start.10
  80.3 1.5 copy-start.4
  80.3 2.8 copy-start.9
  81.9 0.8 copy-start.3
  83.1 2.4 copy-start.2
  85.5 34.5 %all-to-all-start.2 = ((bf16[64,32,256]{2,1,0:T(8,128)(2,1)}), bf16[64,32,256]{2,1,0:T(8,128)(2,1)S(1)}, u32[]{:S(2)}, u32[]{:S(2)}) async-start(bf16[64,32,256]{2,1,0:T(8,128)(2,1)} %bitcast.32), calls=%async_computation.2 | async-start | bytes 2097152 | tf_op jit(solution)/shard_map/all_to_all | solution.py:48
  92.0 257.5 %all-reduce.3.cloned.1.call-start = ((), (), s32[]{:S(2)}) async-start(), calls=%async_computation.3 | async-start | bytes 524288 | tf_op jit(solution)/shard_map/psum | solution.py:38
  94.3 322.1 %all-reduce.5.cloned.1.call-start = ((), (), s32[]{:S(2)}) async-start(), calls=%async_computation.4 | async-start | bytes 4194304 | tf_op jit(solution)/shard_map/psum | solution.py:60
Sparse Core Ops, SparseCore 0:
  98.8 250.6 all-reduce.2
  352.4 63.9 all-reduce.4
where the time goes:
time: 427 us; the launch traced here: 426 us
  waiting for transfers between devices  315 us (74%)
  other arithmetic  25 us (6%)
  local copies, waits for them, and re-layouts  23.5 us (6%)
  blocking collectives  22.2 us (5%)
  between operations  14.2 us (3%)
  matrix products  13.8 us (3%)
  starting transfers between devices  12.4 us (3%)
    psum x1, waiting for transfers between devices, body(): lax.psum(weight_part, ('dom', 'rep')) / jnp.sqrt(jnp.float32(total_rows))  215 us
    psum x1, waiting for transfers between devices, body(): history_grad = lax.psum(grad_table, 'rep')  65.2 us
    all_to_all x1, waiting for transfers between devices, body(): lax.all_to_all(fetched, 'dom', split_axis=0, concat_axis=0, tiled=True)  22.9 us
    all_to_all x1, blocking collectives, body(): lax.all_to_all(requests, 'dom', split_axis=0, concat_axis=0, tiled=True)  22.2 us
    scatter-add x1, other arithmetic, body(): grad_table = grad_table.at[asked_flat].add(arrived_rows.astype(jnp.float32))  14.5 us
    all_to_all x1, waiting for transfers between devices, body(): lax.all_to_all(grad_halo.reshape(owners, slots_per, feature_width), 'dom'...  12.1 us
    gather x1, local copies, waits for them, and re-layouts, body(): fetched = history[asked_ids]  9.86 us
  transfers between devices with their start and end apart: 4, of which 4 were waited for; matrix products, arithmetic and copies ran while one was open for 9% of the time, Pallas kernels for 0%

commit v1 on v0

v1 whole, which is shorter than its diff:
```python
import jax
import jax.numpy as jnp
from jax import lax
from jax.experimental import pallas as pl
from jax.experimental.pallas import tpu as pltpu
from jax.sharding import PartitionSpec as P

BF16, F32, I32 = jnp.bfloat16, jnp.float32, jnp.int32
VMEM = pl.BlockSpec(memory_space=pltpu.VMEM)
SMEM = pl.BlockSpec(memory_space=pltpu.SMEM)
LOW = 4


def vmem_call(kernel, out_shape, in_specs, flops=0, moved=0, scratch=()):
    return pl.pallas_call(
        kernel,
        out_shape=out_shape,
        in_specs=in_specs,
        out_specs=jax.tree.map(lambda _: VMEM, out_shape),
        scratch_shapes=list(scratch),
        compiler_params=pltpu.CompilerParams(vmem_limit_bytes=40 * 1024 * 1024),
        cost_estimate=pl.CostEstimate(flops=flops, bytes_accessed=moved, transcendentals=0),
    )


def as_column(id_row):
    return jnp.broadcast_to(id_row, (128, 128)).T


def gather_kernel(ids_ref, table_ref, out_ref):
    nodes = table_ref.shape[0]
    lane = lax.broadcasted_iota(I32, (256, 128), 1)
    for step in range(out_ref.shape[0] // 256):
        column = jnp.concatenate(
            [as_column(ids_ref[2 * step : 2 * step + 1, :]), as_column(ids_ref[2 * step + 1 : 2 * step + 2, :])], 0
        )
        picks = jnp.concatenate(
            [(column == lane + base).astype(F32).astype(BF16) for base in range(0, nodes, 128)], 1
        )
        rows = jnp.dot(picks, table_ref[...], preferred_element_type=F32)
        out_ref[256 * step : 256 * step + 256, :] = rows.astype(BF16)


def gather_rows(table, ids):
    count, (nodes, width) = ids.shape[0], table.shape
    return vmem_call(
        gather_kernel,
        jax.ShapeDtypeStruct((count, width), BF16),
        [VMEM, VMEM],
        flops=2 * count * nodes * width,
        moved=4 * count * width,
    )(ids.reshape(count // 128, 128), table)


def pack_pair(first, second, part):
    block = slice(128 * (part // 2), 128 * (part // 2) + 128)
    left = lax.broadcasted_iota(I32, (first.shape[0], 128), 1) < 64
    if part % 2 == 0:
        return jnp.where(left, first[:, block], pltpu.roll(second[:, block], 64, 1))
    return jnp.where(left, pltpu.roll(first[:, block], 64, 1), second[:, block])


def pack_halo_kernel(counts_ref, grads_ref, weight_ref, out_ref):
    slots = 32
    row = lax.broadcasted_iota(I32, (slots, 256), 0)
    row8 = lax.broadcasted_iota(I32, (8, 128), 0) // 2
    for half in range(2):

        def one_owner(step, _, half=half):
            owner = step + 32 * half
            start = pl.multiple_of(owner * slots, slots)
            grads = jnp.where(row < counts_ref[0, owner], grads_ref[pl.ds(start, slots), :], 0.0)
            weights = weight_ref[pl.ds(pl.multiple_of(step * 8, 8), 8), 128 * half : 128 * half + 128]
            upper = weights.astype(BF16).astype(F32)
            lower = pltpu.roll(weights - upper, 4, 0)
            for part in range(4):
                tail = jnp.where(row8 == part, upper, jnp.where(row8 == (part + 2) % 4, lower, 0.0))
                message = jnp.concatenate([pack_pair(grads[:16], grads[16:], part), tail], 0)
                out_ref[owner * 4 + part] = message.astype(BF16)
            return 0

        lax.fori_loop(0, 32, one_owner, 0)


def pack_local_kernel(grads_ref, out_ref):
    half = grads_ref.shape[0] // 2
    for base in range(0, half, 64):
        first = grads_ref[base : base + 64, :]
        second = grads_ref[half + base : half + base + 64, :]
        for part in range(4):
            out_ref[part, base : base + 64, :] = pack_pair(first, second, part).astype(BF16)


def add_rows(total, first_ids, second_ids, first_low, second_low, packed):
    high_row = lax.broadcasted_iota(I32, (512, 128), 0)
    left = lax.broadcasted_iota(I32, (512, 128), 1) < 64
    group = jnp.where(left, 0, 1)
    wide = packed.astype(F32)
    turned = pltpu.roll(wide, 64, 1)
    for ids, low, rows in (
        (first_ids, first_low, jnp.where(left, wide, turned)),
        (second_ids, second_low, jnp.where(left, turned, wide)),
    ):
        spread = jnp.concatenate(
            [jnp.where(low == group, rows, 0.0), jnp.where(low == group + 2, rows, 0.0)], 1
        ).astype(BF16)
        picks = jnp.concatenate(
            [(high_row == (ids[i : i + 1, :] & 511)).astype(F32).astype(BF16) for i in range(4)], 1
        )
        total = total + jnp.dot(picks, spread, preferred_element_type=F32)
    return total


def scatter_local_kernel(first_ref, second_ref, first_low_ref, second_low_ref, *refs):
    packed_refs, out_ref = refs[:4], refs[4]
    total = jnp.zeros((512, 256), F32)
    for i, packed_ref in enumerate(packed_refs):
        k, n = slice(4 * i, 4 * i + 4), slice(512 * i, 512 * i + 512)
        total = add_rows(
            total, first_ref[k, :], second_ref[k, :], first_low_ref[n, :], second_low_ref[n, :], packed_ref[...]
        )
    out_ref[...] = total


def scatter_halo_kernel(first_ref, second_ref, first_low_ref, second_low_ref, packed_ref, start_ref, out_ref):
    total = start_ref[...]
    for i in range(8):
        k, n = slice(4 * i, 4 * i + 4), slice(512 * i, 512 * i + 512)
        packed = packed_ref[32 * i : 32 * i + 32, 0:16, :].reshape(512, 128)
        total = add_rows(
            total, first_ref[k, :], second_ref[k, :], first_low_ref[n, :], second_low_ref[n, :], packed
        )
    out_ref[...] = total.astype(BF16)


def unpack_kernel(rep_ref, *refs):
    tables, out_ref = refs[:4], refs[4]
    left = lax.broadcasted_iota(I32, (128, 128), 1) < 64
    for rep in range(4):

        @pl.when(rep_ref[0] == rep)
        def _(rep=rep):
            for low in range(4):
                for base in range(0, 512, 128):
                    block = [
                        tables[(rep - part) % 4][base : base + 128, 128 * (low // 2) : 128 * (low // 2) + 128].astype(F32)
                        for part in range(4)
                    ]
                    for pair in range(2):
                        one, two = block[2 * pair], block[2 * pair + 1]
                        if low % 2 == 0:
                            joined = jnp.where(left, one, pltpu.roll(two, 64, 1))
                        else:
                            joined = jnp.where(left, pltpu.roll(one, 64, 1), two)
                        out_ref[512 * low + base : 512 * low + base + 128, 128 * pair : 128 * pair + 128] = joined


def exchange(x, axes):
    return lax.all_to_all(x, axes, split_axis=0, concat_axis=0, tiled=True)


def from_behind(x, by):
    return lax.ppermute(x, "rep", [(i, (i + by) % 4) for i in range(4)])


def lows(ids):
    return jnp.broadcast_to((ids >> 9).reshape(-1, 1), (ids.size, 128))


def body(history, batch_ids, halo_ids, halo_counts, adj_local, adj_halo, weight, cotangent):
    owners = lax.axis_size("dom")
    replicas = lax.axis_size("rep")
    rep = lax.axis_index("rep")
    batch_rows = batch_ids.shape[0]
    slots = halo_ids.shape[2]
    width = history.shape[1]
    both = ("dom", "rep")

    asked = exchange(halo_ids.reshape(owners, 1, slots), "dom").reshape(owners * slots)
    fetched = gather_rows(history, asked)
    halo_rows = exchange(fetched.reshape(owners, slots, width), "dom").reshape(owners * slots, width)

    mine = jnp.concatenate([asked, batch_ids]).reshape(-1, 128)
    ids = [mine] + [from_behind(mine, by) for by in (1, 2, 3)]
    asked_rows = owners * slots // 128
    local_ids = jnp.stack([i[asked_rows:] for i in ids], 0).reshape(replicas, 2, batch_rows // 2)
    by_age = jnp.stack([i[:asked_rows] for i in ids[::-1]], 0)
    by_rep = jnp.roll(by_age, rep + 1, 0).reshape(replicas, owners, 2, slots // 2).transpose(2, 1, 0, 3)
    local_first, local_second = local_ids[:, 0].reshape(-1, 128), local_ids[:, 1].reshape(-1, 128)
    halo_first, halo_second = by_rep[0].reshape(-1, 128), by_rep[1].reshape(-1, 128)

    inputs = gather_rows(history, batch_ids)
    live = jnp.arange(slots, dtype=I32)[None, :] < halo_counts.reshape(owners, 1)
    live_rows = jnp.where(live.reshape(-1, 1), halo_rows, jnp.zeros((), BF16))
    summed = jnp.dot(adj_local, inputs, preferred_element_type=F32) + jnp.dot(
        adj_halo, live_rows, preferred_element_type=F32
    )
    agg = summed.astype(BF16)
    pre_act = jnp.dot(agg, weight, preferred_element_type=F32)
    gate = jax.nn.sigmoid(pre_act)
    layer_out = (pre_act * gate).astype(BF16)
    grad_pre = (cotangent.astype(F32) * gate * (1.0 + pre_act * (1.0 - gate))).astype(BF16)
    weight_part = lax.dot_general(agg, grad_pre, (((0,), (0,)), ((), ())), preferred_element_type=F32)
    grad_agg = lax.dot_general(grad_pre, weight, (((1,), (1,)), ((), ())), preferred_element_type=F32).astype(BF16)
    grad_halo = lax.dot_general(adj_halo, grad_agg, (((0,), (0,)), ((), ())), preferred_element_type=F32)

    messages = vmem_call(
        pack_halo_kernel,
        jax.ShapeDtypeStruct((owners * replicas, 24, 128), BF16),
        [SMEM, VMEM, VMEM],
        moved=4 * 2**20,
    )(halo_counts, grad_halo, weight_part)
    arrived = exchange(messages, both)

    grad_inputs = lax.dot_general(adj_local, grad_agg, (((0,), (0,)), ((), ())), preferred_element_type=F32)
    packed = vmem_call(
        pack_local_kernel,
        jax.ShapeDtypeStruct((replicas, batch_rows // 2, 128), BF16),
        [VMEM],
        moved=2 * 2**20,
    )(grad_inputs)
    locals_ = [lax.dynamic_index_in_dim(packed, rep, 0, keepdims=False)] + [
        from_behind(lax.dynamic_index_in_dim(packed, (rep + by) % replicas, 0, keepdims=False), by) for by in (1, 2, 3)
    ]
    part_shape = jax.ShapeDtypeStruct((512, 256), F32)
    started = vmem_call(scatter_local_kernel, part_shape, [VMEM] * 8, flops=2 * 4096 * 512 * 256, moved=4 * 2**20)(
        local_first, local_second, lows(local_first), lows(local_second), *locals_
    )
    table = vmem_call(
        scatter_halo_kernel,
        jax.ShapeDtypeStruct((512, 256), BF16),
        [VMEM] * 6,
        flops=2 * 8192 * 512 * 256,
        moved=6 * 2**20,
    )(halo_first, halo_second, lows(halo_first), lows(halo_second), arrived, started)
    tables = [table] + [from_behind(table, by) for by in (1, 2, 3)]
    history_grad = vmem_call(
        unpack_kernel,
        jax.ShapeDtypeStruct(history.shape, F32),
        [SMEM] + [VMEM] * 4,
        moved=4 * 2**20,
    )(rep.reshape(1), *tables)

    tails = jnp.sum(arrived[:, 16:, :].astype(F32), axis=0)
    tails = tails + jnp.roll(tails, 4, 0)
    own = lax.dynamic_slice_in_dim(tails, 2 * rep, 2, 0)
    everyone = exchange(jnp.broadcast_to(own[None], (owners * replicas, 2, 128)), both).reshape(2, 256, 128)
    total_rows = batch_rows * owners * replicas
    grad_weight = jnp.concatenate([everyone[0], everyone[1]], 1) / jnp.sqrt(jnp.float32(total_rows))
    return (layer_out, grad_weight, history_grad)


def solution(mesh):
    return jax.shard_map(
        body,
        mesh=mesh,
        in_specs=(
            P("dom", None),
            P(("dom", "rep")),
            P(("dom", "rep"), None, None),
            P(("dom", "rep"), None),
            P(("dom", "rep"), None),
            P(("dom", "rep"), None),
            P(),
            P(("dom", "rep"), None),
        ),
        out_specs=(P(("dom", "rep"), None), P(), P("dom", None)),
        check_vma=False,
    )
```

time: 427 us -> 170 us (0.40)
  waiting for transfers between devices: 315 us -> 69.6 us
  starting transfers between devices: 12.4 us -> 34.4 us
  other arithmetic: 25 us -> 4.38 us
  Pallas kernels: 0 us -> 18.9 us
  local copies, waits for them, and re-layouts: 23.5 us -> 10.1 us
  between operations: 14.2 us -> 1.04 us
  matrix products: 13.8 us -> 9.12 us
    psum x2 -> x0, waiting for transfers between devices: 280 us -> none  [the longest x1 215 us: body(): lax.psum(weight_part, ('dom', 'rep')) / jnp.sqrt(jnp.float32(total_rows))]
    scatter-add x2 -> x0, other arithmetic: 22.4 us -> none  [the longest x1 14.5 us: body(): grad_table = grad_table.at[asked_flat].add(arrived_rows.astype(jnp.float32))]
    pallas_call x0 -> x7, Pallas kernels: none -> 18.9 us  [the longest x1 5.54 us: body(): vmem_call(pack_halo_kernel, jax.ShapeDtypeStruct((owners * replicas, 24,...]
    all_to_all x2 -> x3, waiting for transfers between devices: 35 us -> 53.5 us  [exchange(): return lax.all_to_all(x, axes, split_axis=0, concat_axis=0, tiled=True)]
    ppermute x0 -> x9, waiting for transfers between devices: none -> 16 us  [from_behind(): return lax.ppermute(x, 'rep', [(i, (i + by) % 4) for i in range(4)])]
    gather x2 -> x0, local copies, waits for them, and re-layouts: 14.8 us -> none  [the longest x1 9.86 us: body(): fetched = history[asked_ids]]
    ppermute x0 -> x9, starting transfers between devices: none -> 12 us  [from_behind(): return lax.ppermute(x, 'rep', [(i, (i + by) % 4) for i in range(4)])]
    all_to_all x2 -> x3, starting transfers between devices: 12.1 us -> 22.3 us  [exchange(): return lax.all_to_all(x, axes, split_axis=0, concat_axis=0, tiled=True)]
  transfers between devices with their start and end apart: 4 -> 12, of which waited for: 4 -> 6; matrix products, arithmetic and copies ran while one was open for 9% -> 4% of each run, Pallas kernels for 0% -> 6%
where the time goes in v1:
time: 170 us
  waiting for transfers between devices  69.6 us (41%)
  starting transfers between devices  34.4 us (20%)
  blocking collectives  22.2 us (13%)
  Pallas kernels  18.9 us (11%)
  local copies, waits for them, and re-layouts  10.1 us (6%)
  matrix products  9.12 us (5%)
  other arithmetic  4.38 us (3%)
    all_to_all x3, waiting for transfers between devices, exchange(): return lax.all_to_all(x, axes, split_axis=0, concat_axis=0, tiled=True)  53.5 us
    all_to_all x3, starting transfers between devices, exchange(): return lax.all_to_all(x, axes, split_axis=0, concat_axis=0, tiled=True)  22.3 us
    all_to_all x1, blocking collectives, exchange(): return lax.all_to_all(x, axes, split_axis=0, concat_axis=0, tiled=True)  22.2 us
    ppermute x9, waiting for transfers between devices, from_behind(): return lax.ppermute(x, 'rep', [(i, (i + by) % 4) for i in range(4)])  16 us
    ppermute x9, starting transfers between devices, from_behind(): return lax.ppermute(x, 'rep', [(i, (i + by) % 4) for i in range(4)])  12 us
    pallas_call x1, Pallas kernels, body(): vmem_call(pack_halo_kernel, jax.ShapeDtypeStruct((owners * replicas, 24,...  5.54 us
    unnamed x28, local copies, waits for them, and re-layouts  5.15 us
    pallas_call x1, Pallas kernels, body(): vmem_call(scatter_halo_kernel, jax.ShapeDtypeStruct((512, 256), BF16), [V...  4.93 us
  transfers between devices with their start and end apart: 12, of which 6 were waited for; matrix products, arithmetic and copies ran while one was open for 4% of the time, Pallas kernels for 6%

profile of v1, /device:TPU:1, one launch (start us, length us, event | category | flops | bytes accessed | tf_op | source)
XLA Modules:
  0.0 169.7 jit_solution(12083805244683002910)
XLA Ops:
  0.6 0.9 copy.36
  1.6 22.2 %all_to_all.20 = s32[64,1,32]{2,1,0:T(1,128)S(1)} all-to-all(s32[64,1,32]{2,1,0:T(1,128)S(1)} %bitcast.81), channel_id=1, replica_groups=mesh['dom'=64,'rep'=4] {'dom'}, dimensions={0} | all-to-all | bytes 16384 | tf_op jit(solution)/shard_map/all_to_all | solution.py:159
  23.7 0.5 broadcast.56
  24.3 0.7 reduce.7
  25.0 0.1 reshape_reshape.3.ids_ref
  25.1 1.2 copy-done.4
  26.3 3.3 %shard_map.104 = bf16[2048,256]{1,0:T(8,128)(2,1)} custom-call(s32[16,128]{1,0:T(8,128)S(1)} %reshape_reshape.3.ids_ref, bf16[2048,256]{1,0:T(8,128)(2,1)S(1)} %copy-done.4), custom_call_target="tpu_custom_call" | custom-call | flops 2147483648 | bytes 2097152 | tf_op jit(solution)/shard_map/pallas_call | solution.py:46
  29.6 5.7 %all-to-all-start.1 = ((bf16[64,32,256]{2,1,0:T(8,128)(2,1)}), bf16[64,32,256]{2,1,0:T(8,128)(2,1)}, u32[]{:S(2)}, u32[]{:S(2)}) async-start(bf16[64,32,256]{2,1,0:T(8,128)(2,1)} %bitcast.3), calls=%async_computation.1 | async-start | bytes 2097152 | tf_op jit(solution)/shard_map/all_to_all | solution.py:159
  35.3 0.1 iota_compare_fusion
  35.4 0.1 lt.66
  35.5 1.2 copy-done.5
  36.7 1.3 shard_map.103
  38.0 25.4 %all-to-all-done.1 = bf16[64,32,256]{2,1,0:T(8,128)(2,1)} async-done(((bf16[64,32,256]{2,1,0:T(8,128)(2,1)}), bf16[64,32,256]{2,1,0:T(8,128)(2,1)}, u32[]{:S(2)}, u32[]{:S(2)}) %all-to-all-start.1) | async-done | bytes 1048608 | tf_op jit(solution)/shard_map/all_to_all | solution.py:159
  63.4 1.5 bitcast_select_fusion
  64.9 3.5 %fusion.3 = f32[256,1024]{1,0:T(8,128)S(1)} fusion(bf16[2048,256]{1,0:T(8,128)(2,1)S(1)} %bitcast_select_fusion, bf16[1024,2048]{1,0:T(8,128)(2,1)} %param.13), kind=kOutput, calls=%fused_computation.38 | convolution fusion | flops 1073741824 | bytes 6291456 | tf_op jit(solution)/shard_map/dot_general | solution.py:195
  68.5 0.8 fusion
  69.2 0.1 copy-done.6
  69.3 0.2 copy-done.8
  69.5 1.5 multiply_convert_fusion
  71.1 0.3 fusion.4.weight_ref
  71.4 0.3 convolution_convert_fusion
  71.7 0.2 copy-done.7
  71.9 1.8 %convolution_bitcast_fusion.grads_ref = f32[2048,256]{1,0:T(8,128)S(1)} fusion(bf16[1024,256]{1,0:T(8,128)(2,1)S(1)} %convolution_convert_fusion, bf16[1024,2048]{1,0:T(8,128)(2,1)S(1)} %copy-done.7), kind=kOutput, calls=%fused_computation | convolution fusion | flops 1073741824 | bytes 6815744 | tf_op jit(solution)/shard_map/dot_general | solution.py:205
  73.7 5.5 %shard_map.105 = bf16[256,24,128]{2,1,0:T(8,128)(2,1)S(1)} custom-call(s32[1,64]{1,0:T(1,128)S(1)} %copy-done.3, f32[2048,256]{1,0:T(8,128)S(1)} %convolution_bitcast_fusion.grads_ref, f32[256,256]{1,0:T(8,128)S(1)} %fusion.4.weight_ref), custom_call_target="tpu_custom_call" | custom-call | bytes 4194304 | tf_op jit(solution)/shard_map/pallas_call | solution.py:207
  79.2 1.1 copy-done.1
  80.4 10.0 %all-to-all-start.2 = ((bf16[256,24,128]{2,1,0:T(8,128)(2,1)}), bf16[256,24,128]{2,1,0:T(8,128)(2,1)}, u32[]{:S(2)}, u32[]{:S(2)}) async-start(bf16[256,24,128]{2,1,0:T(8,128)(2,1)} %copy-done.1), calls=%async_computation.2 | async-start | bytes 3145728 | tf_op jit(solution)/shard_map/all_to_all | solution.py:159
  90.4 0.1 reshape.106
  90.4 1.6 collective-permute-start.2
  92.0 2.4 %collective-permute-start.1 = (s32[24,128]{1,0:T(8,128)S(1)}, s32[24,128]{1,0:T(8,128)S(1)}, u32[]{:S(2)}, u32[]{:S(2)}) collective-permute-start(s32[24,128]{1,0:T(8,128)S(1)} %add_bitcast_fusion), channel_id=1, source_target_pairs={{0,2},{1,3},{2,0},{3,1},{4,6},{5,7},{6,4},{7,5},{8,10},{9,11},{10,... | collective-permute-start | bytes 36872 | tf_op jit(solution)/shard_map/ppermute | solution.py:163
  94.5 1.1 collective-permute-start
  95.6 0.1 stack.31
  95.7 1.2 collective-permute-done.1
  96.9 0.6 collective-permute-done
  97.7 0.4 reshape.108
  98.1 0.1 copy.38
  98.2 0.1 copy.42
  98.3 0.1 shift_right_arithmetic.43
  98.5 0.1 copy.41
  98.6 0.1 shift_right_arithmetic.41
  98.7 0.1 copy.40
  98.8 0.1 reshape_squeeze.13.second_ref
  98.9 0.1 copy.39
  99.0 0.1 reshape_squeeze.12.first_ref
  99.2 0.9 convolution_bitcast_fusion.1.grads_ref
  100.1 0.2 shard_map.106
  100.4 2.4 %collective-permute-start.5 = (bf16[512,128]{1,0:T(8,128)(2,1)S(1)}, bf16[512,128]{1,0:T(8,128)(2,1)S(1)}, u32[]{:S(2)}, u32[]{:S(2)}) collective-permute-start(bf16[512,128]{1,0:T(8,128)(2,1)S(1)} %get-tuple-element.5), channel_id=1, source_target_pairs={{0,3},{1,0},{2,1},{3,2},{4,7},{5,4},{6,5},{7,6},{8,11},{9,8},{10,9... | collective-permute-start | bytes 393224 | tf_op jit(solution)/shard_map/ppermute | solution.py:163
  102.8 0.7 collective-permute-start.3
  103.4 28.2 %all-to-all-done.2.packed_ref = bf16[256,24,128]{2,1,0:T(8,128)(2,1)} async-done(((bf16[256,24,128]{2,1,0:T(8,128)(2,1)}), bf16[256,24,128]{2,1,0:T(8,128)(2,1)}, u32[]{:S(2)}, u32[]{:S(2)}) %all-to-all-start.2) | async-done | bytes 1572896 | tf_op jit(solution)/shard_map/all_to_all | solution.py:159
  131.6 1.3 convert_reduce_fusion
  133.0 0.8 broadcast_in_dim.24
  133.7 6.7 %all-to-all-start.3 = ((f32[256,2,128]{2,1,0:T(2,128)}), f32[256,2,128]{2,1,0:T(2,128)S(1)}, u32[]{:S(2)}, u32[]{:S(2)}) async-start(f32[256,2,128]{2,1,0:T(2,128)} %broadcast_in_dim.24), calls=%async_computation.3 | async-start | bytes 524288 | tf_op jit(solution)/shard_map/all_to_all | solution.py:159
  140.5 0.3 broadcast_in_dim.44.first_low_ref
  140.8 0.3 broadcast_in_dim.45.second_low_ref
  141.1 1.9 %shard_map.107.start_ref = f32[512,256]{1,0:T(8,128)S(1)} custom-call(s32[16,128]{1,0:T(8,128)S(1)} %reshape_squeeze.14.first_ref, s32[16,128]{1,0:T(8,128)S(1)} %reshape_squeeze.15.second_ref, s32[2048,128]{1,0:T(8,128)S(1)} %broadcast_in_dim.44.first_low_ref, s32[2048,128]{1,0:T(8,128)S(1)} %broadcast_in_dim.45.second_low_ref, ...), custom_call_target="tpu_custom_call" | custom-call | flops 1073741824 | bytes 4194304 | tf_op jit(solution)/shard_map/pallas_call | solution.py:226
  143.0 0.6 broadcast_in_dim.42.first_low_ref
  143.6 0.6 broadcast_in_dim.43.second_low_ref
  144.2 4.9 %shard_map.108.refs_0_ = bf16[512,256]{1,0:T(8,128)(2,1)S(1)} custom-call(s32[32,128]{1,0:T(8,128)S(1)} %reshape_squeeze.12.first_ref, s32[32,128]{1,0:T(8,128)S(1)} %reshape_squeeze.13.second_ref, s32[4096,128]{1,0:T(8,128)S(1)} %broadcast_in_dim.42.first_low_ref, s32[4096,128]{1,0:T(8,128)S(1)} %broadcast_in_dim.43.second_low_ref, ...), custom_call_target="tpu_custom_call" | custom-call | flops 2147483648 | bytes 6291456 | tf_op jit(solution)/shard_map/pallas_call | solution.py:229
  149.1 2.7 %collective-permute-start.8 = (bf16[512,256]{1,0:T(8,128)(2,1)S(1)}, bf16[512,256]{1,0:T(8,128)(2,1)S(1)}, u32[]{:S(2)}, u32[]{:S(2)}) collective-permute-start(bf16[512,256]{1,0:T(8,128)(2,1)S(1)} %shard_map.108.refs_0_), channel_id=1, source_target_pairs={{0,3},{1,0},{2,1},{3,2},{4,7},{5,4},{6,5},{7,6},{8,11},{9,8},{10,9... | collective-permute-start | bytes 786440 | tf_op jit(solution)/shard_map/ppermute | solution.py:163
  151.9 0.5 collective-permute-start.7
  152.4 0.6 collective-permute-start.6
  153.0 9.8 %collective-permute-done.8.refs_3_ = bf16[512,256]{1,0:T(8,128)(2,1)S(1)} collective-permute-done((bf16[512,256]{1,0:T(8,128)(2,1)S(1)}, bf16[512,256]{1,0:T(8,128)(2,1)S(1)}, u32[]{:S(2)}, u32[]{:S(2)}) %collective-permute-start.8) | collective-permute-done | bytes 262176 | tf_op jit(solution)/shard_map/ppermute | solution.py:163
  162.8 4.4 %collective-permute-done.6.refs_1_ = bf16[512,256]{1,0:T(8,128)(2,1)S(1)} collective-permute-done((bf16[512,256]{1,0:T(8,128)(2,1)S(1)}, bf16[512,256]{1,0:T(8,128)(2,1)S(1)}, u32[]{:S(2)}, u32[]{:S(2)}) %collective-permute-start.6) | collective-permute-done | bytes 262176 | tf_op jit(solution)/shard_map/ppermute | solution.py:163
  167.2 1.7 shard_map.109
  168.9 0.7 maximum_multiply_fusion
  (44 shorter events, 0.3 us)
Async XLA Ops:
  0.6 67.8 %copy-start = (bf16[1024,1024]{1,0:T(8,128)(2,1)S(1)}, bf16[1024,1024]{1,0:T(8,128)(2,1)}, u32[]{:S(2)}) copy-start(bf16[1024,1024]{1,0:T(8,128)(2,1)} %param.12) | copy-start | bytes 6291460
  25.1 1.2 copy-start.4
  29.6 5.7 %copy-start.3 = (s32[1,64]{1,0:T(1,128)S(1)}, s32[1,64]{1,0:T(1,128)}, u32[]{:S(2)}) copy-start(s32[1,64]{1,0:T(1,128)} %counts_ref.1) | copy-start | bytes 772
  29.6 5.9 %copy-start.2 = (s32[1024]{0:T(1024)S(1)}, s32[1024]{0:T(1024)}, u32[]{:S(2)}) copy-start(s32[1024]{0:T(1024)} %param.9) | copy-start | bytes 12292
  29.6 33.8 %all-to-all-start.1 = ((bf16[64,32,256]{2,1,0:T(8,128)(2,1)}), bf16[64,32,256]{2,1,0:T(8,128)(2,1)}, u32[]{:S(2)}, u32[]{:S(2)}) async-start(bf16[64,32,256]{2,1,0:T(8,128)(2,1)} %bitcast.3), calls=%async_computation.1 | async-start | bytes 2097152 | tf_op jit(solution)/shard_map/all_to_all | solution.py:159
  35.5 1.2 copy-start.5
  68.4 0.9 copy-start.6
  68.4 1.1 copy-start.8
  69.5 2.4 %copy-start.7 = (bf16[1024,2048]{1,0:T(8,128)(2,1)S(1)}, bf16[1024,2048]{1,0:T(8,128)(2,1)}, u32[]{:S(2)}) copy-start(bf16[1024,2048]{1,0:T(8,128)(2,1)} %param.13) | copy-start | bytes 12582916
  79.2 1.1 copy-start.1
  80.4 51.2 %all-to-all-start.2 = ((bf16[256,24,128]{2,1,0:T(8,128)(2,1)}), bf16[256,24,128]{2,1,0:T(8,128)(2,1)}, u32[]{:S(2)}, u32[]{:S(2)}) async-start(bf16[256,24,128]{2,1,0:T(8,128)(2,1)} %copy-done.1), calls=%async_computation.2 | async-start | bytes 3145728 | tf_op jit(solution)/shard_map/all_to_all | solution.py:159
  90.4 5.3 %collective-permute-start.2 = (s32[24,128]{1,0:T(8,128)S(1)}, s32[24,128]{1,0:T(8,128)S(1)}, u32[]{:S(2)}, u32[]{:S(2)}) collective-permute-start(s32[24,128]{1,0:T(8,128)S(1)} %add_bitcast_fusion), channel_id=1, source_target_pairs={{0,1},{1,2},{2,3},{3,0},{4,5},{5,6},{6,7},{7,4},{8,9},{9,10},{10,1... | collective-permute-start | bytes 36872 | tf_op jit(solution)/shard_map/ppermute | solution.py:163
  92.0 4.8 %collective-permute-start.1 = (s32[24,128]{1,0:T(8,128)S(1)}, s32[24,128]{1,0:T(8,128)S(1)}, u32[]{:S(2)}, u32[]{:S(2)}) collective-permute-start(s32[24,128]{1,0:T(8,128)S(1)} %add_bitcast_fusion), channel_id=1, source_target_pairs={{0,2},{1,3},{2,0},{3,1},{4,6},{5,7},{6,4},{7,5},{8,10},{9,11},{10,... | collective-permute-start | bytes 36872 | tf_op jit(solution)/shard_map/ppermute | solution.py:163
  94.5 3.0 %collective-permute-start = (s32[24,128]{1,0:T(8,128)S(1)}, s32[24,128]{1,0:T(8,128)S(1)}, u32[]{:S(2)}, u32[]{:S(2)}) collective-permute-start(s32[24,128]{1,0:T(8,128)S(1)} %add_bitcast_fusion), channel_id=1, source_target_pairs={{0,3},{1,0},{2,1},{3,2},{4,7},{5,4},{6,5},{7,6},{8,11},{9,8},{10,9... | collective-permute-start | bytes 36872 | tf_op jit(solution)/shard_map/ppermute | solution.py:163
  100.4 40.0 %collective-permute-start.5 = (bf16[512,128]{1,0:T(8,128)(2,1)S(1)}, bf16[512,128]{1,0:T(8,128)(2,1)S(1)}, u32[]{:S(2)}, u32[]{:S(2)}) collective-permute-start(bf16[512,128]{1,0:T(8,128)(2,1)S(1)} %get-tuple-element.5), channel_id=1, source_target_pairs={{0,3},{1,0},{2,1},{3,2},{4,7},{5,4},{6,5},{7,6},{8,11},{9,8},{10,9... | collective-permute-start | bytes 393224 | tf_op jit(solution)/shard_map/ppermute | solution.py:163
  102.8 37.7 %collective-permute-start.4 = (bf16[512,128]{1,0:T(8,128)(2,1)S(1)}, bf16[512,128]{1,0:T(8,128)(2,1)S(1)}, u32[]{:S(2)}, u32[]{:S(2)}) collective-permute-start(bf16[512,128]{1,0:T(8,128)(2,1)S(1)} %get-tuple-element.6), channel_id=1, source_target_pairs={{0,2},{1,3},{2,0},{3,1},{4,6},{5,7},{6,4},{7,5},{8,10},{9,11},{10,... | collective-permute-start | bytes 393224 | tf_op jit(solution)/shard_map/ppermute | solution.py:163
  102.8 37.7 %collective-permute-start.3 = (bf16[512,128]{1,0:T(8,128)(2,1)S(1)}, bf16[512,128]{1,0:T(8,128)(2,1)S(1)}, u32[]{:S(2)}, u32[]{:S(2)}) collective-permute-start(bf16[512,128]{1,0:T(8,128)(2,1)S(1)} %get-tuple-element.7), channel_id=1, source_target_pairs={{0,1},{1,2},{2,3},{3,0},{4,5},{5,6},{6,7},{7,4},{8,9},{9,10},{10,1... | collective-permute-start | bytes 393224 | tf_op jit(solution)/shard_map/ppermute | solution.py:163
  133.7 35.2 %all-to-all-start.3 = ((f32[256,2,128]{2,1,0:T(2,128)}), f32[256,2,128]{2,1,0:T(2,128)S(1)}, u32[]{:S(2)}, u32[]{:S(2)}) async-start(f32[256,2,128]{2,1,0:T(2,128)} %broadcast_in_dim.24), calls=%async_computation.3 | async-start | bytes 524288 | tf_op jit(solution)/shard_map/all_to_all | solution.py:159
  149.1 13.6 %collective-permute-start.8 = (bf16[512,256]{1,0:T(8,128)(2,1)S(1)}, bf16[512,256]{1,0:T(8,128)(2,1)S(1)}, u32[]{:S(2)}, u32[]{:S(2)}) collective-permute-start(bf16[512,256]{1,0:T(8,128)(2,1)S(1)} %shard_map.108.refs_0_), channel_id=1, source_target_pairs={{0,3},{1,0},{2,1},{3,2},{4,7},{5,4},{6,5},{7,6},{8,11},{9,8},{10,9... | collective-permute-start | bytes 786440 | tf_op jit(solution)/shard_map/ppermute | solution.py:163
  151.9 10.9 %collective-permute-start.7 = (bf16[512,256]{1,0:T(8,128)(2,1)S(1)}, bf16[512,256]{1,0:T(8,128)(2,1)S(1)}, u32[]{:S(2)}, u32[]{:S(2)}) collective-permute-start(bf16[512,256]{1,0:T(8,128)(2,1)S(1)} %shard_map.108.refs_0_), channel_id=1, source_target_pairs={{0,2},{1,3},{2,0},{3,1},{4,6},{5,7},{6,4},{7,5},{8,10},{9,11},{10,... | collective-permute-start | bytes 786440 | tf_op jit(solution)/shard_map/ppermute | solution.py:163
  152.4 14.8 %collective-permute-start.6 = (bf16[512,256]{1,0:T(8,128)(2,1)S(1)}, bf16[512,256]{1,0:T(8,128)(2,1)S(1)}, u32[]{:S(2)}, u32[]{:S(2)}) collective-permute-start(bf16[512,256]{1,0:T(8,128)(2,1)S(1)} %shard_map.108.refs_0_), channel_id=1, source_target_pairs={{0,1},{1,2},{2,3},{3,0},{4,5},{5,6},{6,7},{7,4},{8,9},{9,10},{10,1... | collective-permute-start | bytes 786440 | tf_op jit(solution)/shard_map/ppermute | solution.py:163
